TPU v7x, 512 devices: a whole 4x4x16 slice. The times are simulated.
512 devices in a mesh: doc: 128 (over y, x_lo, z), term: 4 (over x_hi, core).
Axes of the slice: x: 4 (x_hi: 2, x_lo: 2; x = x_hi * 2 + x_lo), y: 4, z: 16, core: 2. Of those that a mesh axis runs over, the one named last changes fastest.
Arguments:
- tfidf: bfloat16 [4096, 131072], P('term', 'doc'), may hold values from 50 to 1000
- pattern: int32 [32, 1024], P('term', 'doc'), may hold values 0 or 1
- factor_w: bfloat16 [4096, 256], P('term'), may hold values from 0.29882812 to 3
- factor_h: bfloat16 [256, 131072], P(None, 'doc'), may hold values from 0.29882812 to 3
Outputs:
- updated_w: bfloat16 [4096, 256], P('term')
- updated_h: bfloat16 [256, 131072], P(None, 'doc')
All inputs are finite; a program needn't handle non-finite values. No bound on the sum of `pattern` on one device may be relied on, other than what follows from the above.
Results may differ from a plain program's by a relative error of at most 0.0004.
The roundings to bfloat16 on the way count: a program that leaves them out, or rounds other values in their place, can miss the bound.
Values may be sent and summed in bfloat16 or wider, within the bound.
A program may use at most 64 MiB of HBM per device.

v0:
```python
import jax
import jax.numpy as jnp
from jax import lax
from jax.sharding import PartitionSpec as P

BLOCK = 128


def expand(pattern):
    block_rows, block_cols = pattern.shape
    spread = jnp.broadcast_to(pattern[:, None, :, None], (block_rows, BLOCK, block_cols, BLOCK))
    return spread.reshape(block_rows * BLOCK, block_cols * BLOCK)


def contract_first(operand_one, operand_two):
    return lax.dot_general(
        operand_one, operand_two, (((0,), (0,)), ((), ())), preferred_element_type=jnp.float32
    )


def contract_last(operand_one, operand_two):
    return lax.dot_general(
        operand_one, operand_two, (((1,), (1,)), ((), ())), preferred_element_type=jnp.float32
    )


def on_device(tfidf, pattern, factor_w, factor_h):
    masked = tfidf * expand(pattern).astype(jnp.bfloat16)
    gram_part = contract_first(factor_w, factor_w)
    numer_part = contract_first(factor_w, masked)
    gram_w, numerator = lax.psum((gram_part, numer_part), "term")
    denominator = jnp.dot(gram_w.astype(jnp.bfloat16), factor_h, preferred_element_type=jnp.float32)
    new_h = (factor_h.astype(jnp.float32) * numerator / denominator).astype(jnp.bfloat16)
    gram_h_part = contract_last(new_h, new_h)
    term_topic, gram_h = lax.psum((contract_last(masked, new_h), gram_h_part), "doc")
    denominator = jnp.dot(factor_w, gram_h.astype(jnp.bfloat16), preferred_element_type=jnp.float32)
    new_w = (factor_w.astype(jnp.float32) * term_topic / denominator).astype(jnp.bfloat16)
    return (new_w, new_h)


def solution(mesh):
    placed = (P("term", "doc"), P("term", "doc"), P("term", None), P(None, "doc"))
    return jax.shard_map(
        on_device,
        mesh=mesh,
        in_specs=placed,
        out_specs=(P("term", None), P(None, "doc")),
        check_vma=False,
    )
```

profile of v0, /device:TPU:4, one launch (start us, length us, event | category | flops | bytes accessed | tf_op | source)
XLA Modules:
  0.0 1284.5 jit_solution(5472504428020697883)
XLA Ops:
  7.2 0.0 copy-start
  7.2 0.0 all-reduce.5.cloned.1.call-start
  7.2 0.7 convert_element_type.26
  8.0 0.3 broadcast_in_dim.2
  8.3 0.0 copy-done
  8.3 3.6 convolution_bitcast_fusion
  11.9 0.0 copy-start.1
  11.9 0.0 all-reduce.5.cloned.1.call-update
  11.9 0.0 all-reduce.7.cloned.1.call-start
  12.0 0.3 fusion.6
  12.3 0.6 copy-done.1
  12.9 1.0 copy.6
  13.9 18.6 %all-reduce.8 = bf16[256,256]{1,0:T(8,128)(2,1)S(1)} all-reduce(f32[256,256]{1,0:T(8,128)S(1)} %fusion.6), channel_id=1, replica_groups=mesh['doc'=128,'term'=4] {'term'}, use_global_device_ids=true, to_apply=%region_1.0 | all-reduce | flops 65536 | bytes 393216 | tf_op jit(solution)/shard_map/psum | solution.py:31
  32.6 42.7 %all-reduce.5.cloned.1.call-done = f32[256,1024]{0,1:T(8,128)} async-done(((f32[256,1024]{0,1:T(8,128)}), f32[256,1024]{0,1:T(8,128)}) %all-reduce.5.cloned.1.call-update) | async-done | bytes 1048592 | tf_op jit(solution)/shard_map/psum | solution.py:31
  75.3 0.0 copy-start.2
  75.3 2.0 fusion.1
  77.3 0.2 copy-done.2
  77.5 1.8 fusion.3
  79.3 0.0 all-reduce.7.cloned.1.call-update
  79.3 1.0 copy.9
  80.3 0.3 fusion.7
  80.7 611.3 %all-reduce.9 = bf16[256,256]{1,0:T(8,128)(2,1)S(1)} all-reduce(f32[256,256]{1,0:T(8,128)S(1)} %fusion.7), channel_id=1, replica_groups=mesh['doc'=128,'term'=4] {'doc'}, use_global_device_ids=true, to_apply=%region_3.0 | all-reduce | flops 65536 | bytes 393216 | tf_op jit(solution)/shard_map/psum | solution.py:35
  692.0 583.4 %all-reduce.7.cloned.1.call-done = f32[1024,256]{1,0:T(8,128)} async-done(((f32[1024,256]{1,0:T(8,128)}), f32[1024,256]{1,0:T(8,128)}) %all-reduce.7.cloned.1.call-update) | async-done | bytes 1048592 | tf_op jit(solution)/shard_map/psum | solution.py:35
  1275.4 2.3 fusion.2
Async XLA Ops:
  7.2 1.1 copy-start
  7.2 68.1 %all-reduce.5.cloned.1.call-start = ((), (), s32[]{:S(2)}) async-start(), calls=%async_computation | async-start | bytes 2097152 | tf_op jit(solution)/shard_map/psum | solution.py:31
  11.9 1.0 copy-start.1
  11.9 1263.5 %all-reduce.7.cloned.1.call-start = ((), (), s32[]{:S(2)}) async-start(), calls=%async_computation.1 | async-start | bytes 2097152 | tf_op jit(solution)/shard_map/psum | solution.py:35
  75.3 2.2 copy-start.2
Sparse Core Ops, SparseCore 0:
  12.0 63.2 all-reduce.4
  79.4 1195.8 all-reduce.6
where the time goes:
time: 1280 us
  blocking collectives  630 us (49%)
  waiting for transfers between devices  626 us (49%)
  between operations  14.1 us (1%)
    psum x1, blocking collectives, on_device(): lax.psum((contract_last(masked, new_h), gram_h_part), 'doc')  611 us
    psum x1, waiting for transfers between devices, on_device(): lax.psum((contract_last(masked, new_h), gram_h_part), 'doc')  583 us
    psum x1, waiting for transfers between devices, on_device(): gram_w, numerator = lax.psum((gram_part, numer_part), 'term')  42.7 us
  transfers between devices with their start and end apart: 2, of which 2 were waited for; matrix products, arithmetic and copies ran while one was open for 0% of the time, Pallas kernels for 0%

commit v1 on v0

v1 whole, which is shorter than its diff:
```python
import jax
import jax.numpy as jnp
from jax import lax
from jax.experimental import pallas as pl
from jax.experimental.pallas import tpu as pltpu
from jax.sharding import PartitionSpec as P

K = 256
BLOCK = 128
NXY = 8
NZ = 16
MESH = pl.DeviceIdType.MESH
F32 = jnp.float32
BF16 = jnp.bfloat16
LEVELS = 65535.0


def dot_tt(a, b, dims):
    return lax.dot_general(a, b, ((dims[0], dims[1]), ((), ())), preferred_element_type=F32)


def encode(value, peak):
    inv = jnp.where(peak > 0.0, LEVELS / peak, 0.0)
    return ((value * inv + 0.5).astype(jnp.int32) - 32768).astype(jnp.int16)


def decode(code, step):
    return (code.astype(jnp.int32) + 32768).astype(F32) * step


def kernel(
    tf_hbm, pat_ref, w_hbm, h_hbm, outw_hbm, outh_hbm,
    tf, masked, w, h, neww, newh,
    hsend, hrecv, gsend, grecv,
    hcode, hcode_in, hstep, hstep_in, gcode, gcode_in, gstep, gstep_in,
    gram_w, gpart, gxy_in, gz, gz_in, gtile, gfull, gram_h,
    acc, wcode, wcode_in, wstep, wstep_in, zsum, zsum_in, znum, znum_in,
    local_sem, core_s, core_r, x2_s, x2_r, gxy_s, gxy_r, gz_s, gz_r, gt_s, gt_r, gf_s, gf_r,
    wc_s, wc_r, ws_s, ws_r, zs_s, zs_r, zn_s, zn_r, ow_s, ow_r,
):
    doc = lax.axis_index("doc")
    term = lax.axis_index("term")
    z = lax.rem(doc, NZ)
    q = lax.div(doc, NZ)
    xh = lax.div(term, 2)
    c = lax.rem(term, 2)
    oc = 1 - c

    def at_core():
        return {"doc": doc, "term": xh * 2 + oc}

    def at_x2():
        return {"doc": doc, "term": (1 - xh) * 2 + c}

    def at_term(t):
        return {"doc": doc, "term": t}

    def at_xy(p):
        return {"doc": p * NZ + z, "term": term}

    def at_z(p):
        return {"doc": q * NZ + p, "term": term}

    def remote(src, dst, ssem, rsem, device):
        return pltpu.make_async_remote_copy(
            src_ref=src, dst_ref=dst, send_sem=ssem, recv_sem=rsem, device_id=device, device_id_type=MESH
        )

    load_w = pltpu.make_async_copy(w_hbm, w, local_sem.at[0])
    load_tf = pltpu.make_async_copy(tf_hbm, tf, local_sem.at[1])
    load_h = pltpu.make_async_copy(h_hbm, h, local_sem.at[2])
    load_w.start()
    load_tf.start()
    load_h.start()

    barrier = pltpu.get_barrier_semaphore()
    for k in range(1, 4):
        pl.semaphore_signal(barrier, inc=1, device_id=at_term(lax.rem(term + k, 4)), device_id_type=MESH)
    for k in range(1, NXY):
        pl.semaphore_signal(barrier, inc=1, device_id=at_xy(lax.rem(q + k, NXY)), device_id_type=MESH)
    for k in range(1, NZ):
        pl.semaphore_signal(barrier, inc=1, device_id=at_z(lax.rem(z + k, NZ)), device_id_type=MESH)

    load_w.wait()
    wv = w[...]
    gsend[...] = dot_tt(wv, wv, ((0,), (0,))).reshape(2, 128, K)
    load_tf.wait()
    for i in range(8):
        for j in range(8):
            rows, cols = pl.ds(i * BLOCK, BLOCK), pl.ds((j % 4) * BLOCK, BLOCK)
            on = pat_ref[i, j].astype(F32).astype(BF16)
            masked[j // 4, rows, cols] = tf[rows, pl.ds(j * BLOCK, BLOCK)] * on

    hsend[...] = dot_tt(wv, masked[oc], ((0,), (0,)))

    pl.semaphore_wait(barrier, 3 + (NXY - 1) + (NZ - 1))
    sends = []

    g_copy = remote(gsend.at[oc], grecv, core_s.at[0], core_r.at[0], at_core())
    g_copy.start()
    h_copy = remote(hsend, hrecv, core_s.at[1], core_r.at[1], at_core())
    h_copy.start()
    own = dot_tt(wv, masked[c], ((0,), (0,)))

    g_copy.wait_recv()
    part = gsend[c] + grecv[...]
    peak = jnp.max(part, axis=0, keepdims=True)
    gstep[...] = peak / LEVELS
    gcode[...] = encode(part, peak)
    gx = remote(gcode, gcode_in, x2_s.at[0], x2_r.at[0], at_x2())
    gx.start()
    gsx = remote(gstep, gstep_in, x2_s.at[1], x2_r.at[1], at_x2())
    gsx.start()

    h_copy.wait_recv()
    part = own + hrecv[...]
    peak = jnp.max(part, axis=0, keepdims=True)
    hstep[...] = peak / LEVELS
    hcode[...] = encode(part, peak)
    hsx = remote(hstep, hstep_in, x2_s.at[2], x2_r.at[2], at_x2())
    hsx.start()
    hx = remote(hcode, hcode_in, x2_s.at[3], x2_r.at[3], at_x2())
    hx.start()
    sends += [g_copy, h_copy, gx, gsx, hsx, hx]

    gx.wait_recv()
    gsx.wait_recv()
    total = decode(gcode[...], gstep[...]) + decode(gcode_in[...], gstep_in[...])
    gram_w[c] = total.astype(BF16)
    gw_copy = remote(gram_w.at[c], gram_w.at[c], core_s.at[2], core_r.at[2], at_core())
    gw_copy.start()
    load_h.wait()
    gw_copy.wait_recv()
    hv = h[:, pl.ds(pl.multiple_of(c * 512, 512), 512)]
    den = jnp.dot(gram_w[...].reshape(K, K), hv, preferred_element_type=F32)
    hsx.wait_recv()
    hx.wait_recv()
    total = decode(hcode[...], hstep[...]) + decode(hcode_in[...], hstep_in[...])
    newh[c] = (hv.astype(F32) * total / den).astype(BF16)
    nh_copy = remote(newh.at[c], newh.at[c], core_s.at[3], core_r.at[3], at_core())
    nh_copy.start()
    sends += [gw_copy, nh_copy]
    nh_copy.wait_recv()
    store_h = [
        pltpu.make_async_copy(newh.at[i], outh_hbm.at[:, pl.ds(i * 512, 512)], local_sem.at[3 + i]) for i in range(2)
    ]
    for copy in store_h:
        copy.start()

    col = pl.ds(pl.multiple_of(c * 128, 128), 128)
    gpart[...] = dot_tt(newh[0], newh[0, col, :], ((1,), (1,))) + dot_tt(newh[1], newh[1, col, :], ((1,), (1,)))
    gxy = []
    for k in range(1, NXY):
        p = lax.rem(q + k, NXY)
        tile = pl.ds(pl.multiple_of(p * 32 + xh * 16, 16), 16)
        copy = remote(gpart.at[tile], gxy_in.at[q], gxy_s.at[k], gxy_r.at[q], at_xy(p))
        copy.start()
        gxy.append(copy)

    wc, ws = [], []
    for k in range(1, NXY):
        p = lax.rem(q + k, NXY)
        rows = pl.ds(pl.multiple_of(p * 128, 128), 128)
        value = dot_tt(masked[0, rows, :], newh[0], ((1,), (1,))) + dot_tt(masked[1, rows, :], newh[1], ((1,), (1,)))
        peak = jnp.max(value, axis=0, keepdims=True)
        code = encode(value, peak)
        step = peak / LEVELS
        for i in range(2):
            wcode[k, i] = code[:, i * 128 : (i + 1) * 128]
        wstep[k] = step
        cs = remote(wstep.at[k], wstep_in.at[q], ws_s.at[k], ws_r.at[q], at_xy(p))
        cs.start()
        ws.append(cs)
        cc = remote(wcode.at[k], wcode_in.at[q], wc_s.at[k], wc_r.at[q], at_xy(p))
        cc.start()
        wc.append(cc)
    rows = pl.ds(pl.multiple_of(q * 128, 128), 128)
    value = dot_tt(masked[0, rows, :], newh[0], ((1,), (1,))) + dot_tt(masked[1, rows, :], newh[1], ((1,), (1,)))
    acc[0] = value[:, :128]
    acc[1] = value[:, 128:]

    gsum = gpart[pl.ds(pl.multiple_of(q * 32 + xh * 16, 16), 16), :]
    for k in range(1, NXY):
        p = lax.rem(q + NXY - k, NXY)
        remote(gxy_in.at[p], gxy_in.at[p], gxy_s.at[k], gxy_r.at[p], at_xy(p)).wait_recv()
        gsum = gsum + gxy_in[p]
    gz[...] = gsum
    gz_in[z] = gsum
    gzc = []
    for k in (8, 7, 9, 6, 10, 5, 11, 4, 12, 3, 13, 2, 14, 1, 15):
        p = lax.rem(z + k, NZ)
        copy = remote(gz, gz_in.at[z], gz_s.at[k], gz_r.at[z], at_z(p))
        copy.start()
        gzc.append(copy)

    total = acc[...]
    for k in range(1, NXY):
        p = lax.rem(q + NXY - k, NXY)
        remote(wstep_in.at[p], wstep_in.at[p], ws_s.at[k], ws_r.at[p], at_xy(p)).wait_recv()
        remote(wcode_in.at[p], wcode_in.at[p], wc_s.at[k], wc_r.at[p], at_xy(p)).wait_recv()
        step = wstep_in[p]
        total = total + jnp.stack(
            [decode(wcode_in[p, i], step[:, i * 128 : (i + 1) * 128]) for i in range(2)]
        )
    zsum[...] = total.reshape(NZ, 16, 128)
    zsc = []
    for k in (8, 7, 9, 6, 10, 5, 11, 4, 12, 3, 13, 2, 14, 1, 15):
        p = lax.rem(z + k, NZ)
        copy = remote(zsum.at[p], zsum_in.at[z], zs_s.at[k], zs_r.at[z], at_z(p))
        copy.start()
        zsc.append(copy)
    zsum_in[z] = zsum[z]

    for k in range(1, NZ):
        p = lax.rem(z + k, NZ)
        remote(gz, gz_in.at[p], gz_s.at[k], gz_r.at[p], at_z(p)).wait_recv()
    gsum = gz_in[0]
    for p in range(1, NZ):
        gsum = gsum + gz_in[p]
    gtile[q] = gsum.astype(BF16)
    gtc = []
    for k in range(1, NXY):
        p = lax.rem(q + k, NXY)
        copy = remote(gtile.at[q], gtile.at[q], gt_s.at[k], gt_r.at[q], at_xy(p))
        copy.start()
        gtc.append(copy)

    for k in range(1, NZ):
        p = lax.rem(z + k, NZ)
        remote(zsum_in.at[p], zsum_in.at[p], zs_s.at[k], zs_r.at[p], at_z(p)).wait_recv()
    zs = zsum_in[0]
    for p in range(1, NZ):
        zs = zs + zsum_in[p]
    znum[...] = zs
    znc = []
    for k in (8, 7, 9, 6, 10, 5, 11, 4, 12, 3, 13, 2, 14, 1, 15):
        p = lax.rem(z + k, NZ)
        copy = remote(znum, znum_in.at[z], zn_s.at[k], zn_r.at[z], at_z(p))
        copy.start()
        znc.append(copy)
    znum_in[z] = zs

    for k in range(1, NXY):
        p = lax.rem(q + k, NXY)
        remote(gtile.at[p], gtile.at[p], gt_s.at[k], gt_r.at[p], at_xy(p)).wait_recv()
    gfull[term] = gtile[...]
    gfc = []
    for k in range(1, 4):
        t = lax.rem(term + k, 4)
        copy = remote(gtile, gfull.at[term], gf_s.at[k], gf_r.at[term], at_term(t))
        copy.start()
        gfc.append(copy)
    for k in range(1, 4):
        t = lax.rem(term + k, 4)
        remote(gtile, gfull.at[t], gf_s.at[k], gf_r.at[t], at_term(t)).wait_recv()
    for xi in range(2):
        for ci in range(2):
            for p in range(NXY):
                gram_h[pl.ds(p * 32 + xi * 16, 16), pl.ds(ci * 128, 128)] = gfull[xi * 2 + ci, p]
    wrows = w[rows, :]
    den = jnp.dot(wrows, gram_h[...], preferred_element_type=F32)
    scaled = wrows.astype(F32)

    for k in range(1, NZ):
        p = lax.rem(z + k, NZ)
        remote(znum, znum_in.at[p], zn_s.at[k], zn_r.at[p], at_z(p)).wait_recv()
    numer = znum_in[...].reshape(2, 128, 128)
    for i in range(2):
        cols = slice(i * 128, (i + 1) * 128)
        neww[rows, pl.ds(i * 128, 128)] = (scaled[:, cols] * numer[i] / den[:, cols]).astype(BF16)
    owc = []
    for k in range(1, NXY):
        p = lax.rem(q + k, NXY)
        copy = remote(neww.at[rows], neww.at[rows], ow_s.at[k], ow_r.at[q], at_xy(p))
        copy.start()
        owc.append(copy)
    for k in range(1, NXY):
        p = lax.rem(q + k, NXY)
        theirs = neww.at[pl.ds(pl.multiple_of(p * 128, 128), 128)]
        remote(theirs, theirs, ow_s.at[k], ow_r.at[p], at_xy(p)).wait_recv()
    store_w = pltpu.make_async_copy(neww, outw_hbm, local_sem.at[5])
    store_w.start()
    for copy in sends + gxy + ws + wc + gzc + zsc + gtc + znc + gfc + owc:
        copy.wait_send()
    for copy in store_h:
        copy.wait()
    store_w.wait()


def on_device(tfidf, pattern, factor_w, factor_h):
    V = pltpu.VMEM
    i16 = jnp.int16
    scratch = [
        V((1024, 1024), BF16), V((2, 1024, 512), BF16), V((1024, K), BF16), V((K, 1024), BF16),
        V((1024, K), BF16), V((2, K, 512), BF16),
        V((K, 512), F32), V((K, 512), F32), V((2, 128, K), F32), V((128, K), F32),
        V((K, 512), i16), V((K, 512), i16), V((1, 512), F32), V((1, 512), F32),
        V((128, K), i16), V((128, K), i16), V((1, K), F32), V((1, K), F32),
        V((2, 128, K), BF16), V((K, 128), F32), V((NXY, 16, 128), F32), V((16, 128), F32), V((NZ, 16, 128), F32),
        V((NXY, 16, 128), BF16), V((4, NXY, 16, 128), BF16), V((K, K), BF16),
        V((2, 128, 128), F32), V((NXY, 2, 128, 128), i16), V((NXY, 2, 128, 128), i16),
        V((NXY, 1, K), F32), V((NXY, 1, K), F32),
        V((NZ, 16, 128), F32), V((NZ, 16, 128), F32), V((16, 128), F32), V((NZ, 16, 128), F32),
    ]
    D = pltpu.SemaphoreType.DMA
    sems = [D((6,)), D((4,)), D((4,)), D((4,)), D((4,))]
    for n in (NXY, NZ, NXY, 4, NXY, NXY, NZ, NZ, NXY):
        sems += [D((n,)), D((n,))]
    any_space = pl.BlockSpec(memory_space=pl.ANY)
    return pl.pallas_call(
        kernel,
        out_shape=(jax.ShapeDtypeStruct((1024, K), BF16), jax.ShapeDtypeStruct((K, 1024), BF16)),
        in_specs=[any_space, pl.BlockSpec(memory_space=pltpu.SMEM), any_space, any_space],
        out_specs=(any_space, any_space),
        scratch_shapes=scratch + sems,
        compiler_params=pltpu.CompilerParams(
            collective_id=0, has_side_effects=True, vmem_limit_bytes=48 * 1024 * 1024
        ),
    )(tfidf, pattern, factor_w, factor_h)


def solution(mesh):
    placed = (P("term", "doc"), P("term", "doc"), P("term", None), P(None, "doc"))
    return jax.shard_map(
        on_device,
        mesh=mesh,
        in_specs=placed,
        out_specs=(P("term", None), P(None, "doc")),
        check_vma=False,
    )
```

time: 1280 us -> 72.1 us (0.06)
  the two profiles are of different devices: /device:TPU:4 before, /device:TPU:2 now
where the time goes in v1:
time: 72.1 us; the launch traced here: 71.8 us
  Pallas kernels  65.2 us (90%)
  local copies, waits for them, and re-layouts  5.94 us (8%)
    pallas_call x1, Pallas kernels, on_device(): pl.pallas_call(kernel, out_shape=(jax.ShapeDtypeStruct((1024, K), BF16),...  65.2 us
    unnamed x10, local copies, waits for them, and re-layouts  5.94 us

profile of v1, /device:TPU:2, one launch (start us, length us, event | category | flops | bytes accessed | tf_op | source)
XLA Modules:
  0.0 71.8 jit_solution(10505388638048000714)
XLA Ops:
  0.6 0.0 copy-start
  0.6 1.6 %copy-done = bf16[1024,1024]{1,0:T(8,128)(2,1)S(1)} copy-done((bf16[1024,1024]{1,0:T(8,128)(2,1)S(1)}, bf16[1024,1024]{1,0:T(8,128)(2,1)}, u32[]{:S(2)}) %copy-start) | copy-done | bytes 2097176
  2.2 0.0 copy-start.1
  2.2 1.0 %copy-done.1 = bf16[1024,256]{1,0:T(8,128)(2,1)S(1)} copy-done((bf16[1024,256]{1,0:T(8,128)(2,1)S(1)}, bf16[1024,256]{1,0:T(8,128)(2,1)}, u32[]{:S(2)}) %copy-start.1) | copy-done | bytes 524312
  3.3 0.0 copy-start.2
  3.3 1.0 %copy-done.2 = bf16[256,1024]{1,0:T(8,128)(2,1)S(1)} copy-done((bf16[256,1024]{1,0:T(8,128)(2,1)S(1)}, bf16[256,1024]{1,0:T(8,128)(2,1)}, u32[]{:S(2)}) %copy-start.2) | copy-done | bytes 524312
  4.3 0.0 copy-start.3
  4.3 0.7 copy-done.3
  5.0 65.2 %shard_map.59 = (bf16[1024,256]{1,0:T(8,128)(2,1)S(1)}, bf16[256,1024]{1,0:T(8,128)(2,1)S(1)}) custom-call(bf16[1024,1024]{1,0:T(8,128)(2,1)S(1)} %copy-done, s32[8,8]{1,0:T(8,128)S(1)} %copy-done.3, bf16[1024,256]{1,0:T(8,128)(2,1)S(1)} %copy-done.1, bf16[256,1024]{1,0:T(8,128)(2,1)S(1)} %copy-done.2), custom_call_target="tpu_custom_call" | custom-call | tf_op jit(solution)/shard_map/pallas_call | solution.py:310
  70.3 0.8 %copy.8 = bf16[1024,256]{1,0:T(8,128)(2,1)} copy(bf16[1024,256]{1,0:T(8,128)(2,1)S(1)} %get-tuple-element.4) | data formatting | bytes 1048576
  71.0 0.8 %copy.9 = bf16[256,1024]{1,0:T(8,128)(2,1)} copy(bf16[256,1024]{1,0:T(8,128)(2,1)S(1)} %get-tuple-element.5) | data formatting | bytes 1048576
Async XLA Ops:
  0.6 1.6 %copy-start = (bf16[1024,1024]{1,0:T(8,128)(2,1)S(1)}, bf16[1024,1024]{1,0:T(8,128)(2,1)}, u32[]{:S(2)}) copy-start(bf16[1024,1024]{1,0:T(8,128)(2,1)} %tf_hbm.1) | copy-start | bytes 6291460
  2.2 1.0 %copy-start.1 = (bf16[1024,256]{1,0:T(8,128)(2,1)S(1)}, bf16[1024,256]{1,0:T(8,128)(2,1)}, u32[]{:S(2)}) copy-start(bf16[1024,256]{1,0:T(8,128)(2,1)} %w_hbm.1) | copy-start | bytes 1572868
  3.3 1.0 %copy-start.2 = (bf16[256,1024]{1,0:T(8,128)(2,1)S(1)}, bf16[256,1024]{1,0:T(8,128)(2,1)}, u32[]{:S(2)}) copy-start(bf16[256,1024]{1,0:T(8,128)(2,1)} %h_hbm.1) | copy-start | bytes 1572868
  4.3 0.7 copy-start.3

commit v2 on v0

v2 whole, which is shorter than its diff:
```python
import jax
import jax.numpy as jnp
from jax import lax
from jax.experimental import pallas as pl
from jax.experimental.pallas import tpu as pltpu
from jax.sharding import PartitionSpec as P

K = 256
BLOCK = 128
NXY = 8
NZ = 16
MESH = pl.DeviceIdType.MESH
F32 = jnp.float32
BF16 = jnp.bfloat16
I16 = jnp.int16
LEVELS = 65535.0
XY = ((2, 1), (2, 0), (1, 1), (3, 1), (1, 0), (3, 0), (0, 1))
ZS = (8, 7, 9, 6, 10, 5, 11, 4, 12, 3, 13, 2, 14, 1, 15)
NEAR = 9


def dot(a, b, dims):
    return lax.dot_general(a, b, (dims, ((), ())), preferred_element_type=F32)


def encode(value, peak):
    inv = jnp.where(peak > 0.0, LEVELS / peak, 0.0)
    return ((value * inv + 0.5).astype(jnp.int32) - 32768).astype(I16)


def decode(code, step):
    return (code.astype(jnp.int32) + 32768).astype(F32) * step


def kernel(
    tf_hbm, pat_hbm, w_hbm, h_hbm, outw, outh,
    tf, masked, pat, w, wt, h, newh, newht,
    hsend, hrecv, hcode, hcode_in, hstep, hstep_in,
    gsend, grecv, gcode, gcode_in, gstep, gstep_in, gram_w,
    gpart, gxy_in, gz, gz_in, gfull, gram_h, ratio,
    wcode, wcode_in, wstep, wstep_in, own_rel, zsum, zsum_in, znum_in, tiles,
    ready1, ready2,
    load_s, store_s, core_s, core_r, x2_s, x2_r, gxy_s, gxy_r, gz_s, gz_r, gf_s, gf_r,
    wf_s, wf_r, wn_s, wn_r, ws_s, ws_r, zs_s, zs_r, zn_s, zn_r, on_s, on_r, of_s, of_r,
):
    doc = lax.axis_index("doc")
    term = lax.axis_index("term")
    z = lax.rem(doc, NZ)
    q = lax.div(doc, NZ)
    y, xl = lax.div(q, 2), lax.rem(q, 2)
    xh = lax.div(term, 2)
    c = lax.rem(term, 2)
    oc = 1 - c

    def at_term(t):
        return {"doc": doc, "term": t}

    def xy_of(off, sign=1):
        return lax.rem(y + 4 + sign * off[0], 4) * 2 + lax.rem(xl + off[1], 2)

    def at_xy(p):
        return {"doc": p * NZ + z, "term": term}

    def at_z(k):
        return {"doc": q * NZ + lax.rem(z + k + NZ, NZ), "term": term}

    core = at_term(xh * 2 + oc)
    across = at_term((1 - xh) * 2 + c)
    sends = []

    def remote(src, dst, ssem, rsem, device):
        return pltpu.make_async_remote_copy(
            src_ref=src, dst_ref=dst, send_sem=ssem, recv_sem=rsem, device_id=device, device_id_type=MESH
        )

    def send(src, dst, ssem, rsem, device):
        copy = remote(src, dst, ssem, rsem, device)
        copy.start()
        sends.append(copy)
        return copy

    chunks = [oc * 2, oc * 2 + 1, c * 2, c * 2 + 1]
    cols = [pl.ds(pl.multiple_of(g * 256, 256), 256) for g in chunks]
    load_w = pltpu.make_async_copy(w_hbm, w, load_s.at[0])
    load_pat = pltpu.make_async_copy(pat_hbm, pat, load_s.at[1])
    load_h = pltpu.make_async_copy(h_hbm, h, load_s.at[2])
    load_tf = [pltpu.make_async_copy(tf_hbm.at[:, cols[i]], tf.at[:, cols[i]], load_s.at[3 + i]) for i in range(4)]
    load_w.start()
    load_pat.start()
    for copy in load_tf:
        copy.start()
    load_h.start()

    barrier = pltpu.get_barrier_semaphore()
    for off in ((0, 0),) + XY:
        for t in range(4):
            if off != (0, 0) or t:
                pl.semaphore_signal(
                    barrier, inc=1, device_id={"doc": xy_of(off) * NZ + z, "term": lax.rem(term + t, 4)}, device_id_type=MESH
                )
    for k in (-2, 2, -1, 1):
        pl.semaphore_signal(barrier, inc=1, device_id=at_z(k), device_id_type=MESH)

    load_w.wait()
    wt[...] = w[...].T
    gsend[...] = dot(wt[...], w[...], ((1,), (0,))).reshape(2, 128, K)
    load_pat.wait()

    def mask(i):
        load_tf[i].wait()
        for a in range(8):
            for b in range(2):
                rows = pl.ds(a * BLOCK, BLOCK)
                at = pl.ds(pl.multiple_of(chunks[i] * 256 + b * BLOCK, BLOCK), BLOCK)
                on = pat[a, chunks[i] * 2 + b].astype(F32).astype(BF16)
                masked[rows, at] = tf[rows, at] * on

    def numerator_h(i):
        return dot(wt[...], masked[:, cols[i]], ((1,), (0,)))

    mask(0)
    hsend[0] = numerator_h(0)
    pl.semaphore_wait(barrier, 35)
    for k in (-2, 2):
        pl.semaphore_signal(ready1, inc=1, device_id=at_z(k), device_id_type=MESH)

    g_copy = send(gsend.at[oc], grecv, core_s.at[0], core_r.at[0], core)
    h_copy = [send(hsend.at[0], hrecv.at[0], core_s.at[1], core_r.at[1], core)]
    mask(1)
    hsend[1] = numerator_h(1)
    h_copy.append(send(hsend.at[1], hrecv.at[1], core_s.at[2], core_r.at[2], core))

    g_copy.wait_recv()
    part = gsend[c] + grecv[...]
    peak = jnp.max(part, axis=0, keepdims=True)
    gstep[...] = peak / LEVELS
    gcode[...] = encode(part, peak)
    gx = [
        send(gcode, gcode_in, x2_s.at[0], x2_r.at[0], across),
        send(gstep, gstep_in, x2_s.at[1], x2_r.at[1], across),
    ]
    hx = []
    for u in range(2):
        mask(2 + u)
        own = numerator_h(2 + u)
        h_copy[u].wait_recv()
        part = own + hrecv[u]
        peak = jnp.max(part, axis=0, keepdims=True)
        hstep[u] = peak / LEVELS
        hcode[u] = encode(part, peak)
        hx.append(send(hstep.at[u], hstep_in.at[u], x2_s.at[2 + u], x2_r.at[2 + u], across))
        hx.append(send(hcode.at[u], hcode_in.at[u], x2_s.at[4 + u], x2_r.at[4 + u], across))

    for copy in gx:
        copy.wait_recv()
    total = decode(gcode[...], gstep[...]) + decode(gcode_in[...], gstep_in[...])
    gram_w[c] = total.astype(BF16)
    gw = send(gram_w.at[c], gram_w.at[c], core_s.at[3], core_r.at[3], core)
    pl.semaphore_wait(ready1, 2)
    for k in (-4, 4):
        pl.semaphore_signal(ready2, inc=1, device_id=at_z(k), device_id_type=MESH)
    load_h.wait()
    gw.wait_recv()
    stores = []
    nh = []
    for u in range(2):
        hv = h[:, cols[2 + u]]
        den = dot(gram_w[...].reshape(K, K), hv, ((1,), (0,)))
        hx[2 * u].wait_recv()
        hx[2 * u + 1].wait_recv()
        total = decode(hcode[u], hstep[u]) + decode(hcode_in[u], hstep_in[u])
        new = (hv.astype(F32) * total / den).astype(BF16)
        g = chunks[2 + u]
        newh[g] = new
        nh.append(send(newh.at[g], newh.at[g], core_s.at[4 + u], core_r.at[4 + u], core))
        stores.append(pltpu.make_async_copy(newh.at[g], outh.at[:, cols[2 + u]], store_s.at[u]))
        newht[pl.ds(pl.multiple_of(g * 256, 256), 256), :] = new.T

    rows = pl.ds(pl.multiple_of(xh * 128, 128), 128)
    for i in range(2):
        gpart[i] = sum(
            dot(newh[chunks[2 + u], rows, :], newht[pl.ds(pl.multiple_of(chunks[2 + u] * 256, 256), 256), i * 128 : i * 128 + 128], ((1,), (0,)))
            for u in range(2)
        )
    gxy = []
    n = 0
    for off in XY + ((0, 0),):
        p = xy_of(off)
        for dc in range(2):
            if off == (0, 0) and dc == 0:
                continue
            tc = lax.rem(c + dc, 2)
            tile = gpart.at[tc, pl.ds(pl.multiple_of(p * 16, 16), 16)]
            gxy.append(
                send(tile, gxy_in.at[n], gxy_s.at[n], gxy_r.at[n], {"doc": p * NZ + z, "term": xh * 2 + tc})
            )
            n += 1

    for u in range(2):
        g = chunks[u]
        theirs = newh.at[g]
        remote(theirs, theirs, core_s.at[4 + u], core_r.at[4 + u], core).wait_recv()
        newht[pl.ds(pl.multiple_of(g * 256, 256), 256), :] = newh[g].T
        stores.append(pltpu.make_async_copy(theirs, outh.at[:, cols[u]], store_s.at[2 + u]))

    def slot_of(tile):
        return lax.rem(tile + 20 - z, NZ)

    def part_of(p):
        return dot(masked[pl.ds(pl.multiple_of(p * 128, 128), 128), :], newht[...], ((1,), (0,)))

    wf, wn, ws = [], [], []
    for k, off in enumerate(XY):
        p = xy_of(off)
        value = part_of(p)
        peak = jnp.max(value, axis=0, keepdims=True)
        code = encode(value, peak)
        step = peak / LEVELS
        for i in range(2):
            wstep[k, i] = step[:, i * 128 : (i + 1) * 128]
            for b in range(8):
                wcode[k, slot_of(i * 8 + b)] = code[b * 16 : (b + 1) * 16, i * 128 : (i + 1) * 128]
        ws.append(send(wstep.at[k], wstep_in.at[k], ws_s.at[k], ws_r.at[k], at_xy(p)))
        wf.append(send(wcode.at[k, NEAR:], wcode_in.at[k, NEAR:], wf_s.at[k], wf_r.at[k], at_xy(p)))
    for k, off in enumerate(XY):
        wn.append(send(wcode.at[k, :NEAR], wcode_in.at[k, :NEAR], wn_s.at[k], wn_r.at[k], at_xy(xy_of(off))))
    value = part_of(q)
    for i in range(2):
        for b in range(8):
            own_rel[slot_of(i * 8 + b)] = value[b * 16 : (b + 1) * 16, i * 128 : (i + 1) * 128]
    for copy in stores:
        copy.start()

    gsum = gpart[c, pl.ds(pl.multiple_of(q * 16, 16), 16), :]
    for n in range(15):
        gxy[n].wait_recv()
        gsum = gsum + gxy_in[n]
    gz[...] = gsum
    gz_in[z] = gsum
    pl.semaphore_wait(ready2, 2)
    for k in ZS:
        send(gz, gz_in.at[z], gz_s.at[k], gz_r.at[z], at_z(k))

    def sum_xy(slots):
        for s in slots:
            half = lax.div(lax.rem(z + s + 12, NZ), 8)
            total = own_rel[s]
            for k in range(7):
                total = total + decode(wcode_in[k, s], wstep_in[k, half])
            zsum[s] = total

    zs = {}
    for k in range(7):
        ws[k].wait_recv()
        wf[k].wait_recv()
    sum_xy(range(NEAR, NZ))
    for k in ZS[:7]:
        s = (k + 4) % NZ
        zs[s] = send(zsum.at[s], zsum_in.at[s], zs_s.at[s], zs_r.at[s], at_z(k))
    for k in range(7):
        wn[k].wait_recv()
    sum_xy(range(NEAR))
    for k in ZS[7:]:
        s = (k + 4) % NZ
        zs[s] = send(zsum.at[s], zsum_in.at[s], zs_s.at[s], zs_r.at[s], at_z(k))

    for k in range(1, NZ):
        p = lax.rem(z + k, NZ)
        remote(gz, gz_in.at[p], gz_s.at[k], gz_r.at[p], at_z(k)).wait_recv()
    gsum = gz_in[0]
    for p in range(1, NZ):
        gsum = gsum + gz_in[p]
    mine = (xh * NXY + q) * 2 + c
    gfull[mine] = gsum.astype(BF16)
    gf = []
    n = 0
    for off in XY + ((0, 0),):
        p = xy_of(off)
        for dt in (2, 3, 1, 0):
            if off == (0, 0) and dt == 0:
                continue
            device = {"doc": p * NZ + z, "term": lax.rem(term + dt, 4)}
            send(gfull.at[mine], gfull.at[mine], gf_s.at[n], gf_r.at[mine], device)
            n += 1

    total = zsum[4]
    for s in range(NZ):
        if s != 4:
            zs[s].wait_recv()
            total = total + zsum_in[s]
    znum_in[4] = total
    zn = {}
    for k in ZS:
        s = (4 - k) % NZ
        zn[s] = send(znum_in.at[4], znum_in.at[s], zn_s.at[s], zn_r.at[s], at_z(k))

    for off in XY + ((0, 0),):
        p = xy_of(off)
        for dt in (2, 3, 1, 0):
            if off == (0, 0) and dt == 0:
                continue
            t = lax.rem(term + dt, 4)
            at = (lax.div(t, 2) * NXY + p) * 2 + lax.rem(t, 2)
            theirs = gfull.at[at]
            remote(theirs, theirs, gf_s.at[0], gf_r.at[at], at_term(t)).wait_recv()
    for a in range(16):
        for i in range(2):
            gram_h[pl.ds(a * 16, 16), pl.ds(i * 128, 128)] = gfull[a * 2 + i]
    wrows = w[pl.ds(pl.multiple_of(q * 128, 128), 128), :]
    ratio[...] = wrows.astype(F32) / dot(wrows, gram_h[...], ((1,), (0,)))

    def spot(s):
        tile = lax.rem(z + s + 12, NZ)
        return pl.multiple_of(lax.rem(tile, 8) * 16, 16), pl.multiple_of(lax.div(tile, 8) * 128, 128)

    def finish(slots):
        for s in slots:
            row, col = spot(s)
            tiles[q, s] = (ratio[pl.ds(row, 16), pl.ds(col, 128)] * znum_in[s]).astype(BF16)

    for s in range(NEAR):
        if s != 4:
            zn[s].wait_recv()
    finish(range(NEAR))
    on, of = [], []
    for k, off in enumerate(XY):
        src = tiles.at[q, :NEAR]
        on.append(send(src, src, on_s.at[k], on_r.at[q], at_xy(xy_of(off))))
    for s in range(NEAR, NZ):
        zn[s].wait_recv()
    finish(range(NEAR, NZ))
    for k, off in enumerate(XY):
        src = tiles.at[q, NEAR:]
        of.append(send(src, src, of_s.at[k], of_r.at[q], at_xy(xy_of(off))))

    def place(p, slots):
        for s in slots:
            row, col = spot(s)
            outw[pl.ds(pl.multiple_of(p * 128 + row, 16), 16), pl.ds(col, 128)] = tiles[p, s]

    place(q, range(NZ))
    for k, off in enumerate(XY):
        p = xy_of(off)
        theirs = tiles.at[p, :NEAR]
        remote(theirs, theirs, on_s.at[k], on_r.at[p], at_xy(p)).wait_recv()
        place(p, range(NEAR))
    for k, off in enumerate(XY):
        p = xy_of(off)
        theirs = tiles.at[p, NEAR:]
        remote(theirs, theirs, of_s.at[k], of_r.at[p], at_xy(p)).wait_recv()
        place(p, range(NEAR, NZ))
    for copy in sends:
        copy.wait_send()
    for copy in stores:
        copy.wait()


def on_device(tfidf, pattern, factor_w, factor_h):
    V = pltpu.VMEM
    scratch = [
        V((1024, 1024), BF16), V((1024, 1024), BF16), pltpu.SMEM((8, 8), jnp.int32),
        V((1024, K), BF16), V((K, 1024), BF16), V((K, 1024), BF16), V((4, K, 256), BF16), V((1024, K), BF16),
        V((2, K, 256), F32), V((2, K, 256), F32), V((2, K, 256), I16), V((2, K, 256), I16),
        V((2, 1, 256), F32), V((2, 1, 256), F32),
        V((2, 128, K), F32), V((128, K), F32), V((128, K), I16), V((128, K), I16), V((1, K), F32), V((1, K), F32),
        V((2, 128, K), BF16),
        V((2, 128, 128), F32), V((15, 16, 128), F32), V((16, 128), F32), V((NZ, 16, 128), F32),
        V((32, 16, 128), BF16), V((K, K), BF16), V((128, K), F32),
        V((7, NZ, 16, 128), I16), V((7, NZ, 16, 128), I16), V((7, 2, 1, 128), F32), V((7, 2, 1, 128), F32),
        V((NZ, 16, 128), F32), V((NZ, 16, 128), F32), V((NZ, 16, 128), F32), V((NZ, 16, 128), F32),
        V((NXY, NZ, 16, 128), BF16),
    ]
    D = pltpu.SemaphoreType.DMA
    sems = [pltpu.SemaphoreType.REGULAR, pltpu.SemaphoreType.REGULAR, D((7,)), D((4,))]
    for a, b in ((6, 6), (6, 6), (15, 15), (NZ, NZ), (31, 32), (7, 7), (7, 7), (7, 7), (NZ, NZ), (NZ, NZ), (7, 8), (7, 8)):
        sems += [D((a,)), D((b,))]
    hbm = pl.BlockSpec(memory_space=pltpu.HBM)
    return pl.pallas_call(
        kernel,
        out_shape=(jax.ShapeDtypeStruct((1024, K), BF16), jax.ShapeDtypeStruct((K, 1024), BF16)),
        in_specs=[hbm] * 4,
        out_specs=(pl.BlockSpec(memory_space=pltpu.VMEM), pl.BlockSpec(memory_space=pl.ANY)),
        scratch_shapes=scratch + sems,
        compiler_params=pltpu.CompilerParams(
            collective_id=0, has_side_effects=True, vmem_limit_bytes=32 * 1024 * 1024
        ),
    )(*(pltpu.with_memory_space_constraint(a, pltpu.HBM) for a in (tfidf, pattern, factor_w, factor_h)))


def solution(mesh):
    placed = (P("term", "doc"), P("term", "doc"), P("term", None), P(None, "doc"))
    return jax.shard_map(
        on_device,
        mesh=mesh,
        in_specs=placed,
        out_specs=(P("term", None), P(None, "doc")),
        check_vma=False,
    )
```

time: 1280 us -> 63.7 us (0.05)
  the two profiles are of different devices: /device:TPU:4 before, /device:TPU:6 now
where the time goes in v2:
time: 63.7 us; the launch traced here: 63.5 us
  Pallas kernels  61.3 us (96%)
  local copies, waits for them, and re-layouts  1.59 us (2%)
  between operations  0.64 us (1%)
    pallas_call x1, Pallas kernels, on_device(): pl.pallas_call(kernel, out_shape=(jax.ShapeDtypeStruct((1024, K), BF16),...  61.3 us
    unnamed x2, local copies, waits for them, and re-layouts  1.59 us

profile of v2, /device:TPU:6, one launch (start us, length us, event | category | flops | bytes accessed | tf_op | source)
XLA Modules:
  0.0 63.5 jit_solution(9078442370686494446)
XLA Ops:
  0.6 61.3 %shard_map.59 = (bf16[1024,256]{1,0:T(8,128)(2,1)S(1)}, bf16[256,1024]{1,0:T(8,128)(2,1)S(1)}) custom-call(bf16[1024,1024]{1,0:T(8,128)(2,1)} %tf_hbm.1, s32[8,8]{1,0:T(8,128)} %pat_hbm.1, bf16[1024,256]{1,0:T(8,128)(2,1)} %w_hbm.1, bf16[256,1024]{1,0:T(8,128)(2,1)} %h_hbm.1), custom_call_target="tpu_custom_call" | custom-call | tf_op jit(solution)/shard_map/pallas_call | solution.py:378
  62.0 0.8 %copy.8 = bf16[1024,256]{1,0:T(8,128)(2,1)} copy(bf16[1024,256]{1,0:T(8,128)(2,1)S(1)} %get-tuple-element.4) | data formatting | bytes 1048576
  62.8 0.8 %copy.9 = bf16[256,1024]{1,0:T(8,128)(2,1)} copy(bf16[256,1024]{1,0:T(8,128)(2,1)S(1)} %get-tuple-element.5) | data formatting | bytes 1048576

commit v3 on v2

--- a/solution.py
+++ b/solution.py
@@ -38,7 +38,7 @@
     hsend, hrecv, hcode, hcode_in, hstep, hstep_in,
     gsend, grecv, gcode, gcode_in, gstep, gstep_in, gram_w,
     gpart, gxy_in, gz, gz_in, gfull, gram_h, ratio,
-    wcode, wcode_in, wstep, wstep_in, own_rel, zsum, zsum_in, znum_in, tiles,
+    wcode, wcode_in, wstep, wstep_in, acc, zsum, zsum_in, znum_in, tiles,
     ready1, ready2,
     load_s, store_s, core_s, core_r, x2_s, x2_r, gxy_s, gxy_r, gz_s, gz_r, gf_s, gf_r,
     wf_s, wf_r, wn_s, wn_r, ws_s, ws_r, zs_s, zs_r, zn_s, zn_r, on_s, on_r, of_s, of_r,
@@ -55,14 +55,28 @@
     def at_term(t):
         return {"doc": doc, "term": t}
 
-    def xy_of(off, sign=1):
-        return lax.rem(y + 4 + sign * off[0], 4) * 2 + lax.rem(xl + off[1], 2)
+    y_at = [lax.rem(y + i, 4) * 2 for i in range(4)]
+    x_at = [xl, 1 - xl]
+    xy_at = {off: y_at[off[0]] + x_at[off[1]] for off in ((0, 0),) + XY}
+    z_at = [z] + [lax.rem(z + k, NZ) for k in range(1, NZ)]
+    tile_at = [lax.rem(z + s + 12, NZ) for s in range(NZ)]
+    half_at = [lax.div(tile, 8) for tile in tile_at]
+    row_at = [lax.rem(tile, 8) * 16 for tile in tile_at]
+    slot_at = [lax.rem(tile + 20 - z, NZ) for tile in range(NZ)]
+
+    def xy_of(off):
+        return xy_at[off]
 
     def at_xy(p):
         return {"doc": p * NZ + z, "term": term}
 
     def at_z(k):
-        return {"doc": q * NZ + lax.rem(z + k + NZ, NZ), "term": term}
+        return {"doc": q * NZ + z_at[k % NZ], "term": term}
+
+    term_at = [term] + [lax.rem(term + k, 4) for k in range(1, 4)]
+    spread_at = [lax.div(t, 2) * (2 * NXY) + lax.rem(t, 2) for t in term_at]
+    gram_at = {(i, dt): xy_at[off] * 2 + spread_at[dt] for i, off in enumerate(XY + ((0, 0),)) for dt in range(4)}
+    mine = gram_at[len(XY), 0]
 
     core = at_term(xh * 2 + oc)
     across = at_term((1 - xh) * 2 + c)
@@ -73,10 +87,13 @@
             src_ref=src, dst_ref=dst, send_sem=ssem, recv_sem=rsem, device_id=device, device_id_type=MESH
         )
 
-    def send(src, dst, ssem, rsem, device):
+    def send(src, dst, ssem, rsem, device, incoming=None):
         copy = remote(src, dst, ssem, rsem, device)
         copy.start()
         sends.append(copy)
+        if incoming is not None:
+            landing, sem = incoming
+            copy = remote(landing, landing, ssem, sem, device)
         return copy
 
     chunks = [oc * 2, oc * 2 + 1, c * 2, c * 2 + 1]
@@ -92,14 +109,10 @@
     load_h.start()
 
     barrier = pltpu.get_barrier_semaphore()
-    for off in ((0, 0),) + XY:
-        for t in range(4):
-            if off != (0, 0) or t:
-                pl.semaphore_signal(
-                    barrier, inc=1, device_id={"doc": xy_of(off) * NZ + z, "term": lax.rem(term + t, 4)}, device_id_type=MESH
-                )
-    for k in (-2, 2, -1, 1):
-        pl.semaphore_signal(barrier, inc=1, device_id=at_z(k), device_id_type=MESH)
+    greeted = [across] + [at_z(k) for k in (-2, 2)] + [at_xy(xy_of((2, 0)))]
+    greeted += [at_xy(xy_of(off)) for off in ((1, 0), (3, 0), (0, 1))] + [at_z(k) for k in (-1, 1)] + [core]
+    for device in greeted:
+        pl.semaphore_signal(barrier, inc=1, device_id=device, device_id_type=MESH)
 
     load_w.wait()
     wt[...] = w[...].T
@@ -120,9 +133,9 @@
 
     mask(0)
     hsend[0] = numerator_h(0)
-    pl.semaphore_wait(barrier, 35)
-    for k in (-2, 2):
-        pl.semaphore_signal(ready1, inc=1, device_id=at_z(k), device_id_type=MESH)
+    pl.semaphore_wait(barrier, len(greeted))
+    for device in (at_z(-2), at_z(2), at_xy(xy_of((0, 1)))):
+        pl.semaphore_signal(ready1, inc=1, device_id=device, device_id_type=MESH)
 
     g_copy = send(gsend.at[oc], grecv, core_s.at[0], core_r.at[0], core)
     h_copy = [send(hsend.at[0], hrecv.at[0], core_s.at[1], core_r.at[1], core)]
@@ -148,6 +161,10 @@
         peak = jnp.max(part, axis=0, keepdims=True)
         hstep[u] = peak / LEVELS
         hcode[u] = encode(part, peak)
+        if u == 1:
+            pl.semaphore_wait(ready1, 3)
+            for k in (-4, 4):
+                pl.semaphore_signal(ready2, inc=1, device_id=at_z(k), device_id_type=MESH)
         hx.append(send(hstep.at[u], hstep_in.at[u], x2_s.at[2 + u], x2_r.at[2 + u], across))
         hx.append(send(hcode.at[u], hcode_in.at[u], x2_s.at[4 + u], x2_r.at[4 + u], across))
 
@@ -156,9 +173,6 @@
     total = decode(gcode[...], gstep[...]) + decode(gcode_in[...], gstep_in[...])
     gram_w[c] = total.astype(BF16)
     gw = send(gram_w.at[c], gram_w.at[c], core_s.at[3], core_r.at[3], core)
-    pl.semaphore_wait(ready1, 2)
-    for k in (-4, 4):
-        pl.semaphore_signal(ready2, inc=1, device_id=at_z(k), device_id_type=MESH)
     load_h.wait()
     gw.wait_recv()
     stores = []
@@ -172,7 +186,8 @@
         new = (hv.astype(F32) * total / den).astype(BF16)
         g = chunks[2 + u]
         newh[g] = new
-        nh.append(send(newh.at[g], newh.at[g], core_s.at[4 + u], core_r.at[4 + u], core))
+        theirs = newh.at[chunks[u]]
+        nh.append(send(newh.at[g], newh.at[g], core_s.at[4 + u], core_r.at[4 + u], core, (theirs, core_r.at[4 + u])))
         stores.append(pltpu.make_async_copy(newh.at[g], outh.at[:, cols[2 + u]], store_s.at[u]))
         newht[pl.ds(pl.multiple_of(g * 256, 256), 256), :] = new.T
 
@@ -198,36 +213,28 @@
 
     for u in range(2):
         g = chunks[u]
-        theirs = newh.at[g]
-        remote(theirs, theirs, core_s.at[4 + u], core_r.at[4 + u], core).wait_recv()
+        nh[u].wait_recv()
         newht[pl.ds(pl.multiple_of(g * 256, 256), 256), :] = newh[g].T
-        stores.append(pltpu.make_async_copy(theirs, outh.at[:, cols[u]], store_s.at[2 + u]))
-
-    def slot_of(tile):
-        return lax.rem(tile + 20 - z, NZ)
-
-    def part_of(p):
-        return dot(masked[pl.ds(pl.multiple_of(p * 128, 128), 128), :], newht[...], ((1,), (0,)))
-
-    wf, wn, ws = [], [], []
-    for k, off in enumerate(XY):
-        p = xy_of(off)
-        value = part_of(p)
+        stores.append(pltpu.make_async_copy(newh.at[g], outh.at[:, cols[u]], store_s.at[2 + u]))
+
+    for p in range(NXY):
+        value = dot(masked[p * 128 : (p + 1) * 128, :], newht[...], ((1,), (0,)))
+        acc[p] = value
         peak = jnp.max(value, axis=0, keepdims=True)
         code = encode(value, peak)
         step = peak / LEVELS
         for i in range(2):
-            wstep[k, i] = step[:, i * 128 : (i + 1) * 128]
+            wstep[p, i] = step[:, i * 128 : (i + 1) * 128]
             for b in range(8):
-                wcode[k, slot_of(i * 8 + b)] = code[b * 16 : (b + 1) * 16, i * 128 : (i + 1) * 128]
-        ws.append(send(wstep.at[k], wstep_in.at[k], ws_s.at[k], ws_r.at[k], at_xy(p)))
-        wf.append(send(wcode.at[k, NEAR:], wcode_in.at[k, NEAR:], wf_s.at[k], wf_r.at[k], at_xy(p)))
-    for k, off in enumerate(XY):
-        wn.append(send(wcode.at[k, :NEAR], wcode_in.at[k, :NEAR], wn_s.at[k], wn_r.at[k], at_xy(xy_of(off))))
-    value = part_of(q)
-    for i in range(2):
-        for b in range(8):
-            own_rel[slot_of(i * 8 + b)] = value[b * 16 : (b + 1) * 16, i * 128 : (i + 1) * 128]
+                wcode[p, slot_at[i * 8 + b]] = code[b * 16 : (b + 1) * 16, i * 128 : (i + 1) * 128]
+    wf, wn, ws = [], [], []
+    for k, off in enumerate(XY):
+        p = xy_of(off)
+        ws.append(send(wstep.at[p], wstep_in.at[k], ws_s.at[k], ws_r.at[k], at_xy(p)))
+        wf.append(send(wcode.at[p, NEAR:], wcode_in.at[k, NEAR:], wf_s.at[k], wf_r.at[k], at_xy(p)))
+    for k, off in enumerate(XY):
+        p = xy_of(off)
+        wn.append(send(wcode.at[p, :NEAR], wcode_in.at[k, :NEAR], wn_s.at[k], wn_r.at[k], at_xy(p)))
     for copy in stores:
         copy.start()
 
@@ -238,13 +245,15 @@
     gz[...] = gsum
     gz_in[z] = gsum
     pl.semaphore_wait(ready2, 2)
+    gzc = []
     for k in ZS:
-        send(gz, gz_in.at[z], gz_s.at[k], gz_r.at[z], at_z(k))
+        p = z_at[k]
+        gzc.append(send(gz, gz_in.at[z], gz_s.at[k], gz_r.at[z], at_z(k), (gz_in.at[p], gz_r.at[p])))
 
     def sum_xy(slots):
         for s in slots:
-            half = lax.div(lax.rem(z + s + 12, NZ), 8)
-            total = own_rel[s]
+            half = half_at[s]
+            total = acc[q, pl.ds(pl.multiple_of(row_at[s], 16), 16), pl.ds(pl.multiple_of(half * 128, 128), 128)]
             for k in range(7):
                 total = total + decode(wcode_in[k, s], wstep_in[k, half])
             zsum[s] = total
@@ -264,23 +273,23 @@
         s = (k + 4) % NZ
         zs[s] = send(zsum.at[s], zsum_in.at[s], zs_s.at[s], zs_r.at[s], at_z(k))
 
-    for k in range(1, NZ):
-        p = lax.rem(z + k, NZ)
-        remote(gz, gz_in.at[p], gz_s.at[k], gz_r.at[p], at_z(k)).wait_recv()
+    for copy in reversed(gzc):
+        copy.wait_recv()
     gsum = gz_in[0]
     for p in range(1, NZ):
         gsum = gsum + gz_in[p]
-    mine = (xh * NXY + q) * 2 + c
     gfull[mine] = gsum.astype(BF16)
     gf = []
     n = 0
-    for off in XY + ((0, 0),):
+    for p_i, off in enumerate(XY + ((0, 0),)):
         p = xy_of(off)
         for dt in (2, 3, 1, 0):
             if off == (0, 0) and dt == 0:
                 continue
-            device = {"doc": p * NZ + z, "term": lax.rem(term + dt, 4)}
-            send(gfull.at[mine], gfull.at[mine], gf_s.at[n], gf_r.at[mine], device)
+            t = term_at[dt]
+            at = gram_at[p_i, dt]
+            device = {"doc": p * NZ + z, "term": t}
+            gf.append(send(gfull.at[mine], gfull.at[mine], gf_s.at[n], gf_r.at[mine], device, (gfull.at[at], gf_r.at[at])))
             n += 1
 
     total = zsum[4]
@@ -294,15 +303,8 @@
         s = (4 - k) % NZ
         zn[s] = send(znum_in.at[4], znum_in.at[s], zn_s.at[s], zn_r.at[s], at_z(k))
 
-    for off in XY + ((0, 0),):
-        p = xy_of(off)
-        for dt in (2, 3, 1, 0):
-            if off == (0, 0) and dt == 0:
-                continue
-            t = lax.rem(term + dt, 4)
-            at = (lax.div(t, 2) * NXY + p) * 2 + lax.rem(t, 2)
-            theirs = gfull.at[at]
-            remote(theirs, theirs, gf_s.at[0], gf_r.at[at], at_term(t)).wait_recv()
+    for copy in reversed(gf):
+        copy.wait_recv()
     for a in range(16):
         for i in range(2):
             gram_h[pl.ds(a * 16, 16), pl.ds(i * 128, 128)] = gfull[a * 2 + i]
@@ -310,8 +312,7 @@
     ratio[...] = wrows.astype(F32) / dot(wrows, gram_h[...], ((1,), (0,)))
 
     def spot(s):
-        tile = lax.rem(z + s + 12, NZ)
-        return pl.multiple_of(lax.rem(tile, 8) * 16, 16), pl.multiple_of(lax.div(tile, 8) * 128, 128)
+        return pl.multiple_of(row_at[s], 16), pl.multiple_of(half_at[s] * 128, 128)
 
     def finish(slots):
         for s in slots:
@@ -325,13 +326,15 @@
     on, of = [], []
     for k, off in enumerate(XY):
         src = tiles.at[q, :NEAR]
-        on.append(send(src, src, on_s.at[k], on_r.at[q], at_xy(xy_of(off))))
+        p = xy_of(off)
+        on.append(send(src, src, on_s.at[k], on_r.at[q], at_xy(p), (tiles.at[p, :NEAR], on_r.at[p])))
     for s in range(NEAR, NZ):
         zn[s].wait_recv()
     finish(range(NEAR, NZ))
     for k, off in enumerate(XY):
         src = tiles.at[q, NEAR:]
-        of.append(send(src, src, of_s.at[k], of_r.at[q], at_xy(xy_of(off))))
+        p = xy_of(off)
+        of.append(send(src, src, of_s.at[k], of_r.at[q], at_xy(p), (tiles.at[p, NEAR:], of_r.at[p])))
 
     def place(p, slots):
         for s in slots:
@@ -341,13 +344,11 @@
     place(q, range(NZ))
     for k, off in enumerate(XY):
         p = xy_of(off)
-        theirs = tiles.at[p, :NEAR]
-        remote(theirs, theirs, on_s.at[k], on_r.at[p], at_xy(p)).wait_recv()
+        on[k].wait_recv()
         place(p, range(NEAR))
     for k, off in enumerate(XY):
         p = xy_of(off)
-        theirs = tiles.at[p, NEAR:]
-        remote(theirs, theirs, of_s.at[k], of_r.at[p], at_xy(p)).wait_recv()
+        of[k].wait_recv()
         place(p, range(NEAR, NZ))
     for copy in sends:
         copy.wait_send()
@@ -366,8 +367,8 @@
         V((2, 128, K), BF16),
         V((2, 128, 128), F32), V((15, 16, 128), F32), V((16, 128), F32), V((NZ, 16, 128), F32),
         V((32, 16, 128), BF16), V((K, K), BF16), V((128, K), F32),
-        V((7, NZ, 16, 128), I16), V((7, NZ, 16, 128), I16), V((7, 2, 1, 128), F32), V((7, 2, 1, 128), F32),
-        V((NZ, 16, 128), F32), V((NZ, 16, 128), F32), V((NZ, 16, 128), F32), V((NZ, 16, 128), F32),
+        V((NXY, NZ, 16, 128), I16), V((7, NZ, 16, 128), I16), V((NXY, 2, 1, 128), F32), V((7, 2, 1, 128), F32),
+        V((NXY, 128, K), F32), V((NZ, 16, 128), F32), V((NZ, 16, 128), F32), V((NZ, 16, 128), F32),
         V((NXY, NZ, 16, 128), BF16),
     ]
     D = pltpu.SemaphoreType.DMA
@@ -375,7 +376,7 @@
     for a, b in ((6, 6), (6, 6), (15, 15), (NZ, NZ), (31, 32), (7, 7), (7, 7), (7, 7), (NZ, NZ), (NZ, NZ), (7, 8), (7, 8)):
         sems += [D((a,)), D((b,))]
     hbm = pl.BlockSpec(memory_space=pltpu.HBM)
-    return pl.pallas_call(
+    updated = pl.pallas_call(
         kernel,
         out_shape=(jax.ShapeDtypeStruct((1024, K), BF16), jax.ShapeDtypeStruct((K, 1024), BF16)),
         in_specs=[hbm] * 4,
@@ -385,6 +386,21 @@
             collective_id=0, has_side_effects=True, vmem_limit_bytes=32 * 1024 * 1024
         ),
     )(*(pltpu.with_memory_space_constraint(a, pltpu.HBM) for a in (tfidf, pattern, factor_w, factor_h)))
+    return pl.pallas_call(
+        write_out,
+        out_shape=(jax.ShapeDtypeStruct((1024, K), BF16), jax.ShapeDtypeStruct((K, 1024), BF16)),
+        in_specs=[pl.BlockSpec(memory_space=pl.ANY)] * 2,
+        out_specs=(pl.BlockSpec(memory_space=pl.ANY),) * 2,
+        scratch_shapes=[D((2,))],
+    )(*(pltpu.with_memory_space_constraint(a, pltpu.VMEM) for a in updated))
+
+
+def write_out(w, h, outw, outh, sem):
+    copies = [pltpu.make_async_copy(w, outw, sem.at[0]), pltpu.make_async_copy(h, outh, sem.at[1])]
+    for copy in copies:
+        copy.start()
+    for copy in copies:
+        copy.wait()
 
 
 def solution(mesh):

time: 63.7 us -> 60.9 us (0.956)
  the two profiles are of different devices: /device:TPU:6 before, /device:TPU:32 now
where the time goes in v3:
time: 60.9 us; the launch traced here: 60.8 us
  Pallas kernels  60.2 us (99%)
  between operations  0.64 us (1%)
    pallas_call x1, Pallas kernels, on_device(): pl.pallas_call(kernel, out_shape=(jax.ShapeDtypeStruct((1024, K), BF16),...  59.2 us

profile of v3, /device:TPU:32, one launch (start us, length us, event | category | flops | bytes accessed | tf_op | source)
XLA Modules:
  0.0 60.8 jit_solution(8772881103683087816)
XLA Ops:
  0.6 59.2 %shard_map.59 = (bf16[1024,256]{1,0:T(8,128)(2,1)S(1)}, bf16[256,1024]{1,0:T(8,128)(2,1)S(1)}) custom-call(bf16[1024,1024]{1,0:T(8,128)(2,1)} %tf_hbm.1, s32[8,8]{1,0:T(8,128)} %pat_hbm.1, bf16[1024,256]{1,0:T(8,128)(2,1)} %w_hbm.1, bf16[256,1024]{1,0:T(8,128)(2,1)} %h_hbm.1), custom_call_target="tpu_custom_call" | custom-call | tf_op jit(solution)/shard_map/pallas_call | solution.py:379
  59.8 1.0 %shard_map.60 = (bf16[1024,256]{1,0:T(8,128)(2,1)}, bf16[256,1024]{1,0:T(8,128)(2,1)}) custom-call(bf16[1024,256]{1,0:T(8,128)(2,1)S(1)} %get-tuple-element.4.w, bf16[256,1024]{1,0:T(8,128)(2,1)S(1)} %get-tuple-element.5.h), custom_call_target="tpu_custom_call" | custom-call | tf_op jit(solution)/shard_map/pallas_call | solution.py:389

commit v4 on v3

--- a/solution.py
+++ b/solution.py
@@ -39,9 +39,11 @@
     gsend, grecv, gcode, gcode_in, gstep, gstep_in, gram_w,
     gpart, gxy_in, gz, gz_in, gfull, gram_h, ratio,
     wcode, wcode_in, wstep, wstep_in, acc, zsum, zsum_in, znum_in, tiles,
+    gz_step, gz_step_in, zown, zstep, zstep_in, znum_step,
     ready1, ready2,
     load_s, store_s, core_s, core_r, x2_s, x2_r, gxy_s, gxy_r, gz_s, gz_r, gf_s, gf_r,
     wf_s, wf_r, wn_s, wn_r, ws_s, ws_r, zs_s, zs_r, zn_s, zn_r, on_s, on_r, of_s, of_r,
+    gt_s, gt_r, zt_s, zt_r, zm_s, zm_r,
 ):
     doc = lax.axis_index("doc")
     term = lax.axis_index("term")
@@ -117,8 +119,6 @@
     load_w.wait()
     wt[...] = w[...].T
     gsend[...] = dot(wt[...], w[...], ((1,), (0,))).reshape(2, 128, K)
-    load_pat.wait()
-
     def mask(i):
         load_tf[i].wait()
         for a in range(8):
@@ -131,13 +131,14 @@
     def numerator_h(i):
         return dot(wt[...], masked[:, cols[i]], ((1,), (0,)))
 
-    mask(0)
-    hsend[0] = numerator_h(0)
     pl.semaphore_wait(barrier, len(greeted))
     for device in (at_z(-2), at_z(2), at_xy(xy_of((0, 1)))):
         pl.semaphore_signal(ready1, inc=1, device_id=device, device_id_type=MESH)
 
     g_copy = send(gsend.at[oc], grecv, core_s.at[0], core_r.at[0], core)
+    load_pat.wait()
+    mask(0)
+    hsend[0] = numerator_h(0)
     h_copy = [send(hsend.at[0], hrecv.at[0], core_s.at[1], core_r.at[1], core)]
     mask(1)
     hsend[1] = numerator_h(1)
@@ -242,12 +243,17 @@
     for n in range(15):
         gxy[n].wait_recv()
         gsum = gsum + gxy_in[n]
-    gz[...] = gsum
-    gz_in[z] = gsum
+    peak = jnp.max(gsum, axis=0, keepdims=True)
+    gz_step[...] = peak / LEVELS
+    gz_step_in[z] = peak / LEVELS
+    code = encode(gsum, peak)
+    gz[...] = code
+    gz_in[z] = code
     pl.semaphore_wait(ready2, 2)
     gzc = []
     for k in ZS:
         p = z_at[k]
+        gzc.append(send(gz_step, gz_step_in.at[z], gt_s.at[k], gt_r.at[z], at_z(k), (gz_step_in.at[p], gt_r.at[p])))
         gzc.append(send(gz, gz_in.at[z], gz_s.at[k], gz_r.at[z], at_z(k), (gz_in.at[p], gz_r.at[p])))
 
     def sum_xy(slots):
@@ -256,28 +262,35 @@
             total = acc[q, pl.ds(pl.multiple_of(row_at[s], 16), 16), pl.ds(pl.multiple_of(half * 128, 128), 128)]
             for k in range(7):
                 total = total + decode(wcode_in[k, s], wstep_in[k, half])
-            zsum[s] = total
-
-    zs = {}
+            if s == 4:
+                zown[...] = total
+                continue
+            peak = jnp.max(total, axis=0, keepdims=True)
+            zstep[s] = peak / LEVELS
+            zsum[s] = encode(total, peak)
+
+    zs, zt = {}, {}
     for k in range(7):
         ws[k].wait_recv()
         wf[k].wait_recv()
     sum_xy(range(NEAR, NZ))
     for k in ZS[:7]:
         s = (k + 4) % NZ
+        zt[s] = send(zstep.at[s], zstep_in.at[s], zt_s.at[s], zt_r.at[s], at_z(k))
         zs[s] = send(zsum.at[s], zsum_in.at[s], zs_s.at[s], zs_r.at[s], at_z(k))
     for k in range(7):
         wn[k].wait_recv()
     sum_xy(range(NEAR))
     for k in ZS[7:]:
         s = (k + 4) % NZ
+        zt[s] = send(zstep.at[s], zstep_in.at[s], zt_s.at[s], zt_r.at[s], at_z(k))
         zs[s] = send(zsum.at[s], zsum_in.at[s], zs_s.at[s], zs_r.at[s], at_z(k))
 
     for copy in reversed(gzc):
         copy.wait_recv()
-    gsum = gz_in[0]
+    gsum = decode(gz_in[0], gz_step_in[0])
     for p in range(1, NZ):
-        gsum = gsum + gz_in[p]
+        gsum = gsum + decode(gz_in[p], gz_step_in[p])
     gfull[mine] = gsum.astype(BF16)
     gf = []
     n = 0
@@ -292,15 +305,19 @@
             gf.append(send(gfull.at[mine], gfull.at[mine], gf_s.at[n], gf_r.at[mine], device, (gfull.at[at], gf_r.at[at])))
             n += 1
 
-    total = zsum[4]
+    total = zown[...]
     for s in range(NZ):
         if s != 4:
+            zt[s].wait_recv()
             zs[s].wait_recv()
-            total = total + zsum_in[s]
-    znum_in[4] = total
-    zn = {}
+            total = total + decode(zsum_in[s], zstep_in[s])
+    peak = jnp.max(total, axis=0, keepdims=True)
+    znum_in[4] = encode(total, peak)
+    znum_step[4] = peak / LEVELS
+    zn, zm = {}, {}
     for k in ZS:
         s = (4 - k) % NZ
+        zm[s] = send(znum_step.at[4], znum_step.at[s], zm_s.at[s], zm_r.at[s], at_z(k))
         zn[s] = send(znum_in.at[4], znum_in.at[s], zn_s.at[s], zn_r.at[s], at_z(k))
 
     for copy in reversed(gf):
@@ -317,10 +334,11 @@
     def finish(slots):
         for s in slots:
             row, col = spot(s)
-            tiles[q, s] = (ratio[pl.ds(row, 16), pl.ds(col, 128)] * znum_in[s]).astype(BF16)
+            tiles[q, s] = (ratio[pl.ds(row, 16), pl.ds(col, 128)] * decode(znum_in[s], znum_step[s])).astype(BF16)
 
     for s in range(NEAR):
         if s != 4:
+            zm[s].wait_recv()
             zn[s].wait_recv()
     finish(range(NEAR))
     on, of = [], []
@@ -329,6 +347,7 @@
         p = xy_of(off)
         on.append(send(src, src, on_s.at[k], on_r.at[q], at_xy(p), (tiles.at[p, :NEAR], on_r.at[p])))
     for s in range(NEAR, NZ):
+        zm[s].wait_recv()
         zn[s].wait_recv()
     finish(range(NEAR, NZ))
     for k, off in enumerate(XY):
@@ -365,15 +384,16 @@
         V((2, 1, 256), F32), V((2, 1, 256), F32),
         V((2, 128, K), F32), V((128, K), F32), V((128, K), I16), V((128, K), I16), V((1, K), F32), V((1, K), F32),
         V((2, 128, K), BF16),
-        V((2, 128, 128), F32), V((15, 16, 128), F32), V((16, 128), F32), V((NZ, 16, 128), F32),
+        V((2, 128, 128), F32), V((15, 16, 128), F32), V((16, 128), I16), V((NZ, 16, 128), I16),
         V((32, 16, 128), BF16), V((K, K), BF16), V((128, K), F32),
         V((NXY, NZ, 16, 128), I16), V((7, NZ, 16, 128), I16), V((NXY, 2, 1, 128), F32), V((7, 2, 1, 128), F32),
-        V((NXY, 128, K), F32), V((NZ, 16, 128), F32), V((NZ, 16, 128), F32), V((NZ, 16, 128), F32),
+        V((NXY, 128, K), F32), V((NZ, 16, 128), I16), V((NZ, 16, 128), I16), V((NZ, 16, 128), I16),
         V((NXY, NZ, 16, 128), BF16),
+        V((1, 128), F32), V((NZ, 1, 128), F32), V((16, 128), F32), V((NZ, 1, 128), F32), V((NZ, 1, 128), F32), V((NZ, 1, 128), F32),
     ]
     D = pltpu.SemaphoreType.DMA
     sems = [pltpu.SemaphoreType.REGULAR, pltpu.SemaphoreType.REGULAR, D((7,)), D((4,))]
-    for a, b in ((6, 6), (6, 6), (15, 15), (NZ, NZ), (31, 32), (7, 7), (7, 7), (7, 7), (NZ, NZ), (NZ, NZ), (7, 8), (7, 8)):
+    for a, b in ((6, 6), (6, 6), (15, 15), (NZ, NZ), (31, 32), (7, 7), (7, 7), (7, 7), (NZ, NZ), (NZ, NZ), (7, 8), (7, 8), (NZ, NZ), (NZ, NZ), (NZ, NZ)):
         sems += [D((a,)), D((b,))]
     hbm = pl.BlockSpec(memory_space=pltpu.HBM)
     updated = pl.pallas_call(

time: 60.9 us -> 57.5 us (0.944)
  the two profiles are of different devices: /device:TPU:32 before, /device:TPU:2 now
where the time goes in v4:
time: 57.5 us; the launch traced here: 57.4 us
  Pallas kernels  56.7 us (99%)
  between operations  0.64 us (1%)
    pallas_call x1, Pallas kernels, on_device(): pl.pallas_call(kernel, out_shape=(jax.ShapeDtypeStruct((1024, K), BF16),...  55.7 us

profile of v4, /device:TPU:2, one launch (start us, length us, event | category | flops | bytes accessed | tf_op | source)
XLA Modules:
  0.0 57.4 jit_solution(11017978535463250805)
XLA Ops:
  0.6 55.7 %shard_map.59 = (bf16[1024,256]{1,0:T(8,128)(2,1)S(1)}, bf16[256,1024]{1,0:T(8,128)(2,1)S(1)}) custom-call(bf16[1024,1024]{1,0:T(8,128)(2,1)} %tf_hbm.1, s32[8,8]{1,0:T(8,128)} %pat_hbm.1, bf16[1024,256]{1,0:T(8,128)(2,1)} %w_hbm.1, bf16[256,1024]{1,0:T(8,128)(2,1)} %h_hbm.1), custom_call_target="tpu_custom_call" | custom-call | tf_op jit(solution)/shard_map/pallas_call | solution.py:399
  56.4 1.0 %shard_map.60 = (bf16[1024,256]{1,0:T(8,128)(2,1)}, bf16[256,1024]{1,0:T(8,128)(2,1)}) custom-call(bf16[1024,256]{1,0:T(8,128)(2,1)S(1)} %get-tuple-element.4.w, bf16[256,1024]{1,0:T(8,128)(2,1)S(1)} %get-tuple-element.5.h), custom_call_target="tpu_custom_call" | custom-call | tf_op jit(solution)/shard_map/pallas_call | solution.py:409

commit v5 on v4

--- a/solution.py
+++ b/solution.py
@@ -212,14 +212,21 @@
             )
             n += 1
 
+    half = pl.ds(pl.multiple_of(c * 512, 512), 512)
+    for p in range(NXY):
+        acc[p] = dot(masked[p * 128 : (p + 1) * 128, half], newht[half, :], ((1,), (0,)))
+
     for u in range(2):
         g = chunks[u]
         nh[u].wait_recv()
-        newht[pl.ds(pl.multiple_of(g * 256, 256), 256), :] = newh[g].T
+        newht[cols[u], :] = newh[g].T
+        if u == 0:
+            for p in range(NXY):
+                acc[p] += dot(masked[p * 128 : (p + 1) * 128, cols[0]], newht[cols[0], :], ((1,), (0,)))
         stores.append(pltpu.make_async_copy(newh.at[g], outh.at[:, cols[u]], store_s.at[2 + u]))
 
     for p in range(NXY):
-        value = dot(masked[p * 128 : (p + 1) * 128, :], newht[...], ((1,), (0,)))
+        value = acc[p] + dot(masked[p * 128 : (p + 1) * 128, cols[1]], newht[cols[1], :], ((1,), (0,)))
         acc[p] = value
         peak = jnp.max(value, axis=0, keepdims=True)
         code = encode(value, peak)

time: 57.5 us -> 57.1 us (level)
  no operation moved by 1% of the time
where the time goes in v5:
time: 57.1 us; the launch traced here: 57 us
  Pallas kernels  56.4 us (99%)
  between operations  0.64 us (1%)
    pallas_call x1, Pallas kernels, on_device(): pl.pallas_call(kernel, out_shape=(jax.ShapeDtypeStruct((1024, K), BF16),...  55.4 us

profile of v5, /device:TPU:2, one launch (start us, length us, event | category | flops | bytes accessed | tf_op | source)
XLA Modules:
  0.0 57.0 jit_solution(10849481456889806235)
XLA Ops:
  0.6 55.4 %shard_map.59 = (bf16[1024,256]{1,0:T(8,128)(2,1)S(1)}, bf16[256,1024]{1,0:T(8,128)(2,1)S(1)}) custom-call(bf16[1024,1024]{1,0:T(8,128)(2,1)} %tf_hbm.1, s32[8,8]{1,0:T(8,128)} %pat_hbm.1, bf16[1024,256]{1,0:T(8,128)(2,1)} %w_hbm.1, bf16[256,1024]{1,0:T(8,128)(2,1)} %h_hbm.1), custom_call_target="tpu_custom_call" | custom-call | tf_op jit(solution)/shard_map/pallas_call | solution.py:406
  56.0 1.0 %shard_map.60 = (bf16[1024,256]{1,0:T(8,128)(2,1)}, bf16[256,1024]{1,0:T(8,128)(2,1)}) custom-call(bf16[1024,256]{1,0:T(8,128)(2,1)S(1)} %get-tuple-element.4.w, bf16[256,1024]{1,0:T(8,128)(2,1)S(1)} %get-tuple-element.5.h), custom_call_target="tpu_custom_call" | custom-call | tf_op jit(solution)/shard_map/pallas_call | solution.py:416

commit v6 on v5

--- a/solution.py
+++ b/solution.py
@@ -36,7 +36,7 @@
     tf_hbm, pat_hbm, w_hbm, h_hbm, outw, outh,
     tf, masked, pat, w, wt, h, newh, newht,
     hsend, hrecv, hcode, hcode_in, hstep, hstep_in,
-    gsend, grecv, gcode, gcode_in, gstep, gstep_in, gram_w,
+    gsend, grecv, gcode, gcode_in, gstep, gstep_in, gram_w, gram_u,
     gpart, gxy_in, gz, gz_in, gfull, gram_h, ratio,
     wcode, wcode_in, wstep, wstep_in, acc, zsum, zsum_in, znum_in, tiles,
     gz_step, gz_step_in, zown, zstep, zstep_in, znum_step,
@@ -146,9 +146,13 @@
 
     g_copy.wait_recv()
     part = gsend[c] + grecv[...]
-    peak = jnp.max(part, axis=0, keepdims=True)
-    gstep[...] = peak / LEVELS
-    gcode[...] = encode(part, peak)
+    left, right = part[:, :128], part[:, 128:]
+    first = c == 0
+    blocks = (jnp.where(first, left, right), jnp.where(first, right[:64], left.T[64:]))
+    for i, block in enumerate(blocks):
+        peak = jnp.max(block, axis=0, keepdims=True)
+        gstep[i] = peak / LEVELS
+        gcode[i * 128 : i * 128 + block.shape[0]] = encode(block, peak)
     gx = [
         send(gcode, gcode_in, x2_s.at[0], x2_r.at[0], across),
         send(gstep, gstep_in, x2_s.at[1], x2_r.at[1], across),
@@ -171,11 +175,16 @@
 
     for copy in gx:
         copy.wait_recv()
-    total = decode(gcode[...], gstep[...]) + decode(gcode_in[...], gstep_in[...])
-    gram_w[c] = total.astype(BF16)
-    gw = send(gram_w.at[c], gram_w.at[c], core_s.at[3], core_r.at[3], core)
+    for i, at in enumerate((slice(0, 128), slice(128, 192))):
+        gram_u[c, at] = (decode(gcode[at], gstep[i]) + decode(gcode_in[at], gstep_in[i])).astype(BF16)
+    gw = send(gram_u.at[c], gram_u.at[c], core_s.at[3], core_r.at[3], core)
     load_h.wait()
     gw.wait_recv()
+    for i in range(2):
+        gram_w[i, :, i * 128 : i * 128 + 128] = gram_u[i, :128]
+        upper = gram_u[i, 128:]
+        gram_w[0, i * 64 : i * 64 + 64, 128:] = upper
+    gram_w[1, :, :128] = gram_w[0, :, 128:].T
     stores = []
     nh = []
     for u in range(2):
@@ -389,8 +398,8 @@
         V((1024, K), BF16), V((K, 1024), BF16), V((K, 1024), BF16), V((4, K, 256), BF16), V((1024, K), BF16),
         V((2, K, 256), F32), V((2, K, 256), F32), V((2, K, 256), I16), V((2, K, 256), I16),
         V((2, 1, 256), F32), V((2, 1, 256), F32),
-        V((2, 128, K), F32), V((128, K), F32), V((128, K), I16), V((128, K), I16), V((1, K), F32), V((1, K), F32),
-        V((2, 128, K), BF16),
+        V((2, 128, K), F32), V((128, K), F32), V((192, 128), I16), V((192, 128), I16), V((2, 1, 128), F32), V((2, 1, 128), F32),
+        V((2, 128, K), BF16), V((2, 192, 128), BF16),
         V((2, 128, 128), F32), V((15, 16, 128), F32), V((16, 128), I16), V((NZ, 16, 128), I16),
         V((32, 16, 128), BF16), V((K, K), BF16), V((128, K), F32),
         V((NXY, NZ, 16, 128), I16), V((7, NZ, 16, 128), I16), V((NXY, 2, 1, 128), F32), V((7, 2, 1, 128), F32),

time: 57.1 us -> 56.8 us (level)
  no operation moved by 1% of the time
where the time goes in v6:
time: 56.8 us; the launch traced here: 56.7 us
  Pallas kernels  56 us (99%)
  between operations  0.64 us (1%)
    pallas_call x1, Pallas kernels, on_device(): pl.pallas_call(kernel, out_shape=(jax.ShapeDtypeStruct((1024, K), BF16),...  55 us

profile of v6, /device:TPU:2, one launch (start us, length us, event | category | flops | bytes accessed | tf_op | source)
XLA Modules:
  0.0 56.7 jit_solution(1985784735039103196)
XLA Ops:
  0.6 55.0 %shard_map.59 = (bf16[1024,256]{1,0:T(8,128)(2,1)S(1)}, bf16[256,1024]{1,0:T(8,128)(2,1)S(1)}) custom-call(bf16[1024,1024]{1,0:T(8,128)(2,1)} %tf_hbm.1, s32[8,8]{1,0:T(8,128)} %pat_hbm.1, bf16[1024,256]{1,0:T(8,128)(2,1)} %w_hbm.1, bf16[256,1024]{1,0:T(8,128)(2,1)} %h_hbm.1), custom_call_target="tpu_custom_call" | custom-call | tf_op jit(solution)/shard_map/pallas_call | solution.py:415
  55.7 1.0 %shard_map.60 = (bf16[1024,256]{1,0:T(8,128)(2,1)}, bf16[256,1024]{1,0:T(8,128)(2,1)}) custom-call(bf16[1024,256]{1,0:T(8,128)(2,1)S(1)} %get-tuple-element.4.w, bf16[256,1024]{1,0:T(8,128)(2,1)S(1)} %get-tuple-element.5.h), custom_call_target="tpu_custom_call" | custom-call | tf_op jit(solution)/shard_map/pallas_call | solution.py:425
